TPU v7x, 32 devices: a whole 2x2x4 slice. The times are simulated.
32 devices in a mesh: member: 8 (over y, x, core), tile: 4 (over z).
Axes of the slice: x: 2, y: 2, z: 4, core: 2. Of those that a mesh axis runs over, the one named last changes fastest.
Arguments:
- innovations: bfloat16 [8, 4, 256, 256], P('member', None, None, 'tile'), may hold values from -6 to 6
- obs_column: int32 [4, 256], P(None, 'tile'), may hold values from 0 to 511
- physics: float32 [4, 256, 256], replicated, as said below
- diffusion: float32 [256], replicated, may hold values from 0.05 to 0.24
- anomalies: bfloat16 [8, 256, 16, 128], P('member', None, 'tile'), may hold values from -6 to 6
- modes: float32 [256, 16], replicated, may hold values from -3 to 3
- bands: int32 [16], replicated, may hold values from 1 to 8
Outputs:
- gradient: float32 [8, 256, 16, 128], P('member', None, 'tile')
Inputs may be any that keep to these rules, and one draw needn't show every extreme that they name: `obs_column`: index c = x * 128 + y of an observed column within its tile's 4 by 128 columns; indices may repeat. `physics`: each step's matrix has a dominant diagonal near 0.6.
All inputs are finite; a program needn't handle non-finite values.
Results may differ from a plain program's by a relative error of at most 0.0003.
Values sent between devices are 32-bit elements; how exact they have to be, the bound alone decides.
A program may use at most 64 MiB of HBM per device.

v0:
```python
import jax
import jax.numpy as jnp
from jax import lax
from jax.sharding import PartitionSpec as P

STEPS = 4


def padded_2(block, sides, width):
    for axis, dim in sides:
        count = lax.axis_size(axis)
        forward = [(i, i + 1) for i in range(count - 1)]
        forward.append((count - 1, 0))
        backward = [(target, source) for source, target in forward]
        low = lax.ppermute(
            lax.slice_in_dim(block, block.shape[dim] - width, None, axis=dim), axis, forward
        )
        high = lax.ppermute(lax.slice_in_dim(block, 0, width, axis=dim), axis, backward)
        block = jnp.concatenate([low, block, high], axis=dim)
    return block


def smooth_modes(coeffs, bands):
    length = coeffs.shape[-1]
    padded = jnp.pad(coeffs, ((0, 0), (0, 0), (8, 8)))
    total = jnp.zeros(coeffs.shape, jnp.float32)
    for offset in range(-8, 9):
        weight = (jnp.abs(jnp.int32(offset)) <= bands).astype(jnp.float32)
        total = total + weight[:, None, None] * padded[:, :, 8 + offset : 8 + offset + length]
    return total / (2 * bands + 1).astype(jnp.float32)[:, None, None]


def column_physics(matrix, field):
    return jnp.einsum("rs,rxy->sxy", matrix, field, precision=lax.Precision.HIGHEST)


def diffuse(padded, nu):
    center = padded[:, 1:-1]
    ypad = jnp.pad(center, ((0, 0), (0, 0), (1, 1)))
    beside_all = padded[:, 2:] + padded[:, :-2] + ypad[:, :, 2:] + ypad[:, :, :-2]
    return center + nu[:, None, None] * (beside_all - 4.0 * center)


def per_device(innovations, obs_column, physics, diffusion, anomalies, modes, bands):
    members = lax.axis_size("member")
    spread = anomalies[0].astype(jnp.float32)
    state, width_x, width_y = spread.shape
    columns = jnp.arange(width_x * width_y, dtype=jnp.int32)
    lam = jnp.zeros((state, width_x, width_y), jnp.float32)
    for step in range(STEPS - 1, -1, -1):
        local = jnp.einsum("sk,sxy->kxy", modes, spread * lam, precision=lax.Precision.HIGHEST)
        coeffs = lax.psum(local, "member") / jnp.float32(members - 1)
        moved = column_physics(physics[step], lam)
        padded = padded_2(moved, (("tile", 1),), 1)
        spread_out = diffuse(padded, diffusion)
        smooth = smooth_modes(coeffs, bands)
        lifted = jnp.einsum("sk,kxy->sxy", modes, smooth, precision=lax.Precision.HIGHEST)
        onehot = (obs_column[step][:, None] == columns[None, :]).astype(jnp.float32)
        forcing = jnp.dot(
            innovations[0, step].astype(jnp.float32), onehot, precision=lax.Precision.HIGHEST
        )
        forcing = forcing.reshape(state, width_x, width_y)
        lam = spread_out + spread * lifted + forcing
    return lam[None]


def solution(mesh):
    in_specs = (
        P("member", None, None, "tile"),
        P(None, "tile"),
        P(),
        P(),
        P("member", None, "tile", None),
        P(),
        P(),
    )
    out_specs = P("member", None, "tile", None)
    return jax.shard_map(
        per_device, mesh=mesh, in_specs=in_specs, out_specs=out_specs, check_vma=False
    )
```

profile of v0, /device:TPU:0, one launch (start us, length us, event | category | flops | bytes accessed | tf_op | source)
XLA Modules:
  0.0 125.3 jit_solution(12900686982437782464)
XLA Ops:
  0.0 0.0 copy-start
  0.0 1.5 %convolution_bitcast_fusion.7 = f32[256,4,128]{0,2,1:T(8,128)S(1)} fusion(f32[4,256,256]{2,1,0:T(8,128)} %param.9), kind=kOutput, calls=%fused_computation.15 | convolution fusion | flops 402653184 | bytes 786432 | tf_op jit(solution)/shard_map/rs,rxy->sxy/dot_general | solution.py:34
  1.6 0.0 copy-start.2
  1.6 0.0 copy-start.5
  1.6 5.1 %collective-permute-start = (f32[256,1,128]{0,2,1:T(8,128)S(1)}, f32[256,1,128]{0,2,1:T(8,128)S(1)}, u32[]{:S(2)}, u32[]{:S(2)}) collective-permute-start(f32[256,1,128]{0,2,1:T(8,128)S(1)} %get-tuple-element.11), channel_id=1, source_target_pairs={{1,0},{2,1},{3,2},{0,3},{5,4},{6,5},{7,6},{4,7},{9,8},{10,9},{11,1... | collective-permute-start | bytes 393224 | tf_op jit(solution)/shard_map/ppermute | solution.py:18
  6.7 0.0 collective-permute-start.1
  6.7 0.0 copy-done.5
  6.7 0.2 copy.8
  6.9 0.0 copy-start.4
  6.9 0.6 convolution_bitcast_fusion.11
  7.5 24.2 %psum.28 = f32[16,4,128]{2,0,1:T(8,128)S(1)} all-reduce(f32[16,4,128]{2,0,1:T(8,128)S(1)} %convolution_bitcast_fusion.11), channel_id=1, replica_groups=mesh['member'=8,'tile'=4] {'member'}, use_global_device_ids=true, to_apply=%region_0.0 | all-reduce | flops 8192 | bytes 65536 | tf_op jit(solution)/shard_map/psum | solution.py:52
  31.8 0.3 fusion.47
  32.1 0.3 fusion.48
  32.5 0.3 fusion.49
  32.8 0.3 fusion.50
  33.2 0.0 collective-permute-done
  33.2 0.0 collective-permute-done.1
  33.2 0.0 copy-start.7
  33.2 0.6 copy-done.6
  33.8 0.1 copy-done.7
  33.9 0.7 copy-done.8
  34.6 2.1 %fusion.1 = f32[256,4,128]{0,2,1:T(8,128)S(1)} fusion(f32[256,4,128]{0,2,1:T(8,128)S(1)} %bitcast.145, f32[256,4,128]{0,2,1:T(8,128)S(1)} %convolution_bitcast_fusion.7, f32[256,1,128]{0,2,1:T(8,128)} %copy-done.7, f32[256,1,128]{0,2,1:T(8,128)} %copy-done.6, bf16[1,256,4,128]{1,3,2,0:T(8,128)(2,1)S(1)} %copy.8, f32[256]{0:T(256)S(1)} %copy-done.8, ...), kind=kOutput, calls=%fused_computation.17 | convolution fusion | flops 27148288 | bytes 2180736 | tf_op jit(solution)/shard_map/sk,kxy->sxy/dot_general | solution.py:57
  36.7 0.6 convolution_bitcast_fusion.6
  37.3 0.6 convolution_bitcast_fusion.10
  37.8 0.7 fusion.255
  38.5 3.2 %collective-permute-start.2 = (f32[256,1,128]{0,2,1:T(8,128)}, f32[256,1,128]{0,2,1:T(8,128)}, u32[]{:S(2)}, u32[]{:S(2)}) collective-permute-start(f32[256,1,128]{0,2,1:T(8,128)} %get-tuple-element.9), channel_id=1, source_target_pairs={{1,0},{2,1},{3,2},{0,3},{5,4},{6,5},{7,6},{4,7},{9,8},{10,9},{11,1... | collective-permute-start | bytes 393224 | tf_op jit(solution)/shard_map/ppermute | solution.py:18
  41.8 0.0 collective-permute-start.3
  41.8 22.7 %psum.29 = f32[16,4,128]{2,0,1:T(8,128)S(1)} all-reduce(f32[16,4,128]{2,0,1:T(8,128)S(1)} %convolution_bitcast_fusion.10), channel_id=1, replica_groups=mesh['member'=8,'tile'=4] {'member'}, use_global_device_ids=true, to_apply=%region_1.2 | all-reduce | flops 8192 | bytes 65536 | tf_op jit(solution)/shard_map/psum | solution.py:52
  64.5 0.0 collective-permute-done.2
  64.5 0.0 collective-permute-done.3
  64.6 2.0 %fusion.3 = f32[256,4,128]{0,2,1:T(8,128)S(1)} fusion(f32[256,4,128]{0,2,1:T(8,128)S(1)} %bitcast.144, f32[256,4,128]{0,2,1:T(8,128)S(1)} %convolution_bitcast_fusion.6, f32[256,1,128]{0,2,1:T(8,128)} %collective-permute-done.3, f32[256,1,128]{0,2,1:T(8,128)} %collective-permute-done.2, bf16[1,256,4,128]{1,3,2,0:T(8,128)(2,1)S(1)} %copy.8, ...), kind=kOutput, calls=%fused_computation.19 | convolution fusion | flops 27148288 | bytes 2180736 | tf_op jit(solution)/shard_map/sk,kxy->sxy/dot_general | solution.py:57
  66.6 0.6 convolution_bitcast_fusion.5
  67.1 0.6 convolution_bitcast_fusion.9
  67.8 3.5 %collective-permute-start.4 = (f32[256,1,128]{0,2,1:T(8,128)S(1)}, f32[256,1,128]{0,2,1:T(8,128)S(1)}, u32[]{:S(2)}, u32[]{:S(2)}) collective-permute-start(f32[256,1,128]{0,2,1:T(8,128)S(1)} %get-tuple-element.7), channel_id=1, source_target_pairs={{1,0},{2,1},{3,2},{0,3},{5,4},{6,5},{7,6},{4,7},{9,8},{10,9},{11,1... | collective-permute-start | bytes 393224 | tf_op jit(solution)/shard_map/ppermute | solution.py:18
  71.2 0.0 collective-permute-start.5
  71.2 22.7 %psum.30 = f32[16,4,128]{2,0,1:T(8,128)S(1)} all-reduce(f32[16,4,128]{2,0,1:T(8,128)S(1)} %convolution_bitcast_fusion.9), channel_id=1, replica_groups=mesh['member'=8,'tile'=4] {'member'}, use_global_device_ids=true, to_apply=%region_2.3 | all-reduce | flops 8192 | bytes 65536 | tf_op jit(solution)/shard_map/psum | solution.py:52
  94.0 0.0 collective-permute-done.4
  94.0 0.0 collective-permute-done.5
  94.0 1.9 %fusion.5 = f32[256,4,128]{0,2,1:T(8,128)S(1)} fusion(f32[256,4,128]{0,2,1:T(8,128)S(1)} %bitcast.143, f32[256,4,128]{0,2,1:T(8,128)S(1)} %convolution_bitcast_fusion.5, f32[256,1,128]{0,2,1:T(8,128)} %collective-permute-done.5, f32[256,1,128]{0,2,1:T(8,128)S(1)} %collective-permute-done.4, bf16[1,256,4,128]{1,3,2,0:T(8,128)(2,1)S(1)} %copy.8, ...), kind=kOutput, calls=%fused_computation.21 | convolution fusion | flops 27148288 | bytes 2180736 | tf_op jit(solution)/shard_map/sk,kxy->sxy/dot_general | solution.py:57
  95.9 0.6 convolution_bitcast_fusion.4
  96.5 0.6 convolution_bitcast_fusion.8
  97.1 3.5 %collective-permute-start.6 = (f32[256,1,128]{0,2,1:T(8,128)S(1)}, f32[256,1,128]{0,2,1:T(8,128)S(1)}, u32[]{:S(2)}, u32[]{:S(2)}) collective-permute-start(f32[256,1,128]{0,2,1:T(8,128)S(1)} %get-tuple-element.5), channel_id=1, source_target_pairs={{1,0},{2,1},{3,2},{0,3},{5,4},{6,5},{7,6},{4,7},{9,8},{10,9},{11,1... | collective-permute-start | bytes 393224 | tf_op jit(solution)/shard_map/ppermute | solution.py:18
  100.6 0.0 collective-permute-start.7
  100.6 22.6 %psum.31 = f32[16,4,128]{2,0,1:T(8,128)S(1)} all-reduce(f32[16,4,128]{2,0,1:T(8,128)S(1)} %convolution_bitcast_fusion.8), channel_id=1, replica_groups=mesh['member'=8,'tile'=4] {'member'}, use_global_device_ids=true, to_apply=%region_3.4 | all-reduce | flops 8192 | bytes 65536 | tf_op jit(solution)/shard_map/psum | solution.py:52
  123.3 0.0 collective-permute-done.6
  123.3 0.0 collective-permute-done.7
  123.3 1.0 fusion.8
  124.3 1.0 copy.13
  (20 shorter events, 0.1 us)
Async XLA Ops:
  0.0 6.9 %copy-start = (f32[256,16]{0,1:T(8,128)S(1)}, f32[256,16]{0,1:T(8,128)}, u32[]{:S(2)}) copy-start(f32[256,16]{0,1:T(8,128)} %param.12) | copy-start | bytes 49156
  1.6 5.2 %copy-start.2 = (bf16[1,256,4,128]{3,2,1,0:T(4,128)(2,1)S(1)}, bf16[1,256,4,128]{3,2,1,0:T(4,128)(2,1)}, u32[]{:S(2)}) copy-start(bf16[1,256,4,128]{3,2,1,0:T(4,128)(2,1)} %param.11) | copy-start | bytes 786436
  1.6 5.1 %copy-start.5 = (s32[16]{0:T(128)S(1)}, s32[16]{0:T(128)}, u32[]{:S(2)}) copy-start(s32[16]{0:T(128)} %param.13) | copy-start | bytes 196
  1.6 31.6 %collective-permute-start = (f32[256,1,128]{0,2,1:T(8,128)S(1)}, f32[256,1,128]{0,2,1:T(8,128)S(1)}, u32[]{:S(2)}, u32[]{:S(2)}) collective-permute-start(f32[256,1,128]{0,2,1:T(8,128)S(1)} %get-tuple-element.11), channel_id=1, source_target_pairs={{1,0},{2,1},{3,2},{0,3},{5,4},{6,5},{7,6},{4,7},{9,8},{10,9},{11,1... | collective-permute-start | bytes 393224 | tf_op jit(solution)/shard_map/ppermute | solution.py:18
  6.7 26.5 %collective-permute-start.1 = (f32[256,1,128]{0,2,1:T(8,128)S(1)}, f32[256,1,128]{0,2,1:T(8,128)S(1)}, u32[]{:S(2)}, u32[]{:S(2)}) collective-permute-start(f32[256,1,128]{0,2,1:T(8,128)S(1)} %get-tuple-element.12), channel_id=1, source_target_pairs={{0,1},{1,2},{2,3},{3,0},{4,5},{5,6},{6,7},{7,4},{8,9},{9,10},{10,1... | collective-permute-start | bytes 393224 | tf_op jit(solution)/shard_map/ppermute | solution.py:15
  6.9 24.8 %copy-start.4 = (s32[4,64]{1,0:T(4,128)S(1)}, s32[4,64]{1,0:T(4,128)}, u32[]{:S(2)}) copy-start(s32[4,64]{1,0:T(4,128)} %param.8) | copy-start | bytes 3076
  7.5 24.3 %copy-start.3 = (bf16[1,4,256,64]{2,3,1,0:T(8,128)(2,1)S(1)}, bf16[1,4,256,64]{2,3,1,0:T(8,128)(2,1)}, u32[]{:S(2)}) copy-start(bf16[1,4,256,64]{2,3,1,0:T(8,128)(2,1)} %param.7) | copy-start | bytes 393220
  33.2 0.6 copy-start.6
  33.2 0.7 copy-start.7
  33.9 0.7 copy-start.8
  34.6 2.1 %copy-start.1 = (f32[4,256,256]{2,1,0:T(8,128)S(1)}, f32[4,256,256]{2,1,0:T(8,128)}, u32[]{:S(2)}) copy-start(f32[4,256,256]{2,1,0:T(8,128)} %param.9) | copy-start | bytes 3145732
  38.5 26.0 %collective-permute-start.2 = (f32[256,1,128]{0,2,1:T(8,128)}, f32[256,1,128]{0,2,1:T(8,128)}, u32[]{:S(2)}, u32[]{:S(2)}) collective-permute-start(f32[256,1,128]{0,2,1:T(8,128)} %get-tuple-element.9), channel_id=1, source_target_pairs={{1,0},{2,1},{3,2},{0,3},{5,4},{6,5},{7,6},{4,7},{9,8},{10,9},{11,1... | collective-permute-start | bytes 393224 | tf_op jit(solution)/shard_map/ppermute | solution.py:18
  41.8 22.8 %collective-permute-start.3 = (f32[256,1,128]{0,2,1:T(8,128)}, f32[256,1,128]{0,2,1:T(8,128)}, u32[]{:S(2)}, u32[]{:S(2)}) collective-permute-start(f32[256,1,128]{0,2,1:T(8,128)} %get-tuple-element.10), channel_id=1, source_target_pairs={{0,1},{1,2},{2,3},{3,0},{4,5},{5,6},{6,7},{7,4},{8,9},{9,10},{10,1... | collective-permute-start | bytes 393224 | tf_op jit(solution)/shard_map/ppermute | solution.py:15
  67.8 26.2 %collective-permute-start.4 = (f32[256,1,128]{0,2,1:T(8,128)S(1)}, f32[256,1,128]{0,2,1:T(8,128)S(1)}, u32[]{:S(2)}, u32[]{:S(2)}) collective-permute-start(f32[256,1,128]{0,2,1:T(8,128)S(1)} %get-tuple-element.7), channel_id=1, source_target_pairs={{1,0},{2,1},{3,2},{0,3},{5,4},{6,5},{7,6},{4,7},{9,8},{10,9},{11,1... | collective-permute-start | bytes 393224 | tf_op jit(solution)/shard_map/ppermute | solution.py:18
  71.2 22.8 %collective-permute-start.5 = (f32[256,1,128]{0,2,1:T(8,128)S(1)}, f32[256,1,128]{0,2,1:T(8,128)}, u32[]{:S(2)}, u32[]{:S(2)}) collective-permute-start(f32[256,1,128]{0,2,1:T(8,128)S(1)} %get-tuple-element.8), channel_id=1, source_target_pairs={{0,1},{1,2},{2,3},{3,0},{4,5},{5,6},{6,7},{7,4},{8,9},{9,10},{10,1... | collective-permute-start | bytes 393224 | tf_op jit(solution)/shard_map/ppermute | solution.py:15
  97.1 26.1 %collective-permute-start.6 = (f32[256,1,128]{0,2,1:T(8,128)S(1)}, f32[256,1,128]{0,2,1:T(8,128)S(1)}, u32[]{:S(2)}, u32[]{:S(2)}) collective-permute-start(f32[256,1,128]{0,2,1:T(8,128)S(1)} %get-tuple-element.5), channel_id=1, source_target_pairs={{1,0},{2,1},{3,2},{0,3},{5,4},{6,5},{7,6},{4,7},{9,8},{10,9},{11,1... | collective-permute-start | bytes 393224 | tf_op jit(solution)/shard_map/ppermute | solution.py:18
  100.6 22.7 %collective-permute-start.7 = (f32[256,1,128]{0,2,1:T(8,128)S(1)}, f32[256,1,128]{0,2,1:T(8,128)S(1)}, u32[]{:S(2)}, u32[]{:S(2)}) collective-permute-start(f32[256,1,128]{0,2,1:T(8,128)S(1)} %get-tuple-element.6), channel_id=1, source_target_pairs={{0,1},{1,2},{2,3},{3,0},{4,5},{5,6},{6,7},{7,4},{8,9},{9,10},{10,1... | collective-permute-start | bytes 393224 | tf_op jit(solution)/shard_map/ppermute | solution.py:15
where the time goes:
time: 126 us; the launch traced here: 125 us
  blocking collectives  92.3 us (73%)
  starting transfers between devices  15.3 us (12%)
  matrix products  14 us (11%)
  local copies, waits for them, and re-layouts  3.34 us (3%)
    psum x4, blocking collectives, per_device(): coeffs = lax.psum(local, 'member') / jnp.float32(members - 1)  92.3 us
    ppermute x4, starting transfers between devices, padded_2(): lax.ppermute(lax.slice_in_dim(block, 0, width, axis=dim), axis, backward)  15.3 us
    dot_general x4, matrix products, per_device(): jnp.einsum('sk,kxy->sxy', modes, smooth, precision=lax.Precision.HIGHEST)  7.03 us
    dot_general x4, matrix products, column_physics(): jnp.einsum('rs,rxy->sxy', matrix, field, precision=lax.Precision.HIGHEST)  3.29 us
  transfers between devices with their start and end apart: 8, of which 0 were waited for; matrix products, arithmetic and copies ran while one was open for 2% of the time, Pallas kernels for 0%

commit v1 on v0

v1 whole, which is shorter than its diff:
```python
import functools

import jax
import jax.numpy as jnp
from jax import lax
from jax.experimental import pallas as pl
from jax.experimental.pallas import tpu as pltpu
from jax.sharding import PartitionSpec as P

REACH = 8
MESH = pl.DeviceIdType.MESH
F32 = jnp.float32
BF16 = jnp.bfloat16


def split(x):
    hi = x.astype(BF16)
    return hi, (x - hi.astype(F32)).astype(BF16)


def dot(a, b):
    return jnp.dot(a, b, preferred_element_type=F32)


def stacked(x):
    hi, lo = split(x)
    return jnp.concatenate([hi, lo, hi], axis=0)


def spread_obs(profile, obs_row, first, count):
    shape = (count, obs_row.shape[-1])
    column = lax.broadcasted_iota(jnp.int32, shape, 0) + first
    onehot = jnp.where(column == obs_row, 1.0, 0.0).astype(BF16)
    return lax.dot_general(
        profile, onehot, (((0,), (1,)), ((), ())), preferred_element_type=F32
    )


def kernel(
    members, tiles, bands_ref, obs_ref, diff_ref, modes_ref, phys_ref, innov_ref, anom_ref,
    out_ref,
    phys, innov, anom, anom32, weight, field, nu_ref, lift_w, proj_w, smooth_w,
    edge, edge_obs, u_ref, q_ref, total,
    local_sem, edge_send, edge_recv, obs_send, obs_recv, u_send, u_recv, q_send, q_recv,
):
    steps, obs, state = innov.shape
    ny = anom.shape[1]
    nx = anom.shape[0] // state
    modes = modes_ref.shape[0]
    rounds = steps - 1
    me = lax.axis_index("member")
    tile = lax.axis_index("tile")
    after = lax.rem(tile + 1, tiles)
    before = lax.rem(tile + tiles - 1, tiles)

    get_innov = pltpu.make_async_copy(innov_ref.at[0], innov, local_sem.at[0])
    get_phys = pltpu.make_async_copy(phys_ref.at[pl.ds(0, rounds)], phys, local_sem.at[1])
    get_anom = pltpu.make_async_copy(anom_ref, anom, local_sem.at[2])
    get_innov.start()
    get_anom.start()
    get_phys.start()

    barrier = pltpu.get_barrier_semaphore()
    for near in (before, after):
        pl.semaphore_signal(barrier, inc=1, device_id={"tile": near}, device_id_type=MESH)
    for j in range(1, members):
        peer = lax.rem(me + j, members)
        pl.semaphore_signal(barrier, inc=1, device_id={"member": peer}, device_id_type=MESH)

    get_innov.wait()
    edge[0] = innov[rounds].astype(F32)
    pl.semaphore_wait(barrier, members + 1)

    edge_copies = []
    for side, near in ((0, after), (1, before)):
        edge_copies.append(pltpu.make_async_remote_copy(
            edge.at[0], edge.at[1 + side], edge_send.at[side], edge_recv.at[side],
            device_id={"tile": near}, device_id_type=MESH))
        edge_copies.append(pltpu.make_async_remote_copy(
            obs_ref, edge_obs.at[side], obs_send.at[side], obs_recv.at[side],
            device_id={"tile": near}, device_id_type=MESH))
    for copy in edge_copies:
        copy.start()

    obs_all = obs_ref[...]
    field[...] = spread_obs(innov[rounds], obs_all[rounds : rounds + 1], 0, nx * ny)

    hi, lo = split(modes_ref[...])
    proj_w[...] = jnp.concatenate([hi, lo], axis=0)
    parts = jnp.concatenate([hi, hi, lo], axis=0).astype(F32)
    pad = lift_w.shape[1] - 3 * modes
    lift_w[...] = jnp.concatenate([parts, jnp.zeros((pad, state), F32)], axis=0).T.astype(BF16)

    get_anom.wait()
    anom32[...] = anom[...].astype(F32)

    def project_and_send(r):
        hi_cols, lo_cols = [], []
        for x in range(nx):
            cols = slice(x * ny, (x + 1) * ny)
            a, b = split(anom32[pl.ds(x, state, stride=nx), :] * field[:, cols])
            hi_cols.append(a)
            lo_cols.append(b)
        both = dot(proj_w[...], jnp.concatenate(hi_cols, axis=1))
        low = dot(proj_w[0:modes], jnp.concatenate(lo_cols, axis=1))
        q_ref[r, 0] = both[0:modes] + both[modes:] + low
        copies = []
        for j in range(1, members):
            copies.append(pltpu.make_async_remote_copy(
                q_ref.at[r, 0], q_ref.at[r, j], q_send.at[r, j], q_recv.at[r, j],
                device_id={"member": lax.rem(me + j, members)}, device_id_type=MESH))
        for copy in copies:
            copy.start()
        return copies

    pending = project_and_send(0)

    row = lax.broadcasted_iota(jnp.int32, (modes, ny), 0)
    lane = lax.broadcasted_iota(jnp.int32, (modes, ny), 1)
    bands = jnp.zeros((modes, ny), jnp.int32)
    for k in range(modes):
        bands = jnp.where(row == k, bands_ref[k], bands)
    scale = 1.0 / ((2 * bands + 1).astype(F32) * F32(members - 1))
    for i, d in enumerate(range(-REACH, REACH + 1)):
        ok = (abs(d) <= bands) & (lane + d >= 0) & (lane + d < ny)
        smooth_w[i] = jnp.where(ok, scale, 0.0)

    nu_ref[...] = jnp.broadcast_to(diff_ref[...], (ny, state)).T

    get_phys.wait()

    def physics_weights(t):
        hi, lo = split(phys[t].T)
        weight[t] = jnp.concatenate([hi, hi, lo], axis=1)

    physics_weights(rounds - 1)

    def smoothed(r):
        rows = []
        for x in range(nx):
            cols = slice(x * ny, (x + 1) * ny)
            q = total[:, cols]
            acc = smooth_w[REACH] * q
            for i, d in enumerate(range(-REACH, REACH + 1)):
                if d != 0:
                    acc = acc + smooth_w[i] * pltpu.roll(q, (-d) % ny, 1)
            rows.append(acc)
        return jnp.concatenate(rows, axis=1)

    lane_y = lax.broadcasted_iota(jnp.int32, (state, ny), 1)

    for r in range(rounds):
        t = rounds - 1 - r
        halo = []
        if r > 0:
            outer = jnp.concatenate([field[:, 0:ny], field[:, (nx - 1) * ny :]], axis=1)
            u = dot(weight[t], stacked(outer))
            u_ref[r, 1] = u[:, 0:ny]
            u_ref[r, nx] = u[:, ny:]
            halo = [
                pltpu.make_async_remote_copy(
                    u_ref.at[r, 1], u_ref.at[r, nx + 1], u_send.at[r, 0], u_recv.at[r, 0],
                    device_id={"tile": before}, device_id_type=MESH),
                pltpu.make_async_remote_copy(
                    u_ref.at[r, nx], u_ref.at[r, 0], u_send.at[r, 1], u_recv.at[r, 1],
                    device_id={"tile": after}, device_id_type=MESH),
            ]
            for copy in halo:
                copy.start()
            pending = project_and_send(r)
            u = dot(weight[t], stacked(field[:, ny : (nx - 1) * ny]))
            for x in range(1, nx - 1):
                u_ref[r, 1 + x] = u[:, (x - 1) * ny : x * ny]
        else:
            u = dot(weight[t], stacked(field[...]))
            for x in range(nx):
                u_ref[r, 1 + x] = u[:, x * ny : (x + 1) * ny]
        if t > 0:
            physics_weights(t - 1)
        nu = nu_ref[...]
        field[...] = spread_obs(innov[t], obs_all[t : t + 1], 0, nx * ny)
        for x in range(nx):
            cols = slice(x * ny, (x + 1) * ny)
            mid = u_ref[r, 1 + x]
            beside = jnp.where(lane_y == 0, 0.0, pltpu.roll(mid, 1, 1))
            beside = beside + jnp.where(lane_y == ny - 1, 0.0, pltpu.roll(mid, ny - 1, 1))
            if x > 0:
                beside = beside + u_ref[r, x]
            if x < nx - 1:
                beside = beside + u_ref[r, x + 2]
            field[:, cols] += mid + nu * (beside - 4.0 * mid)
        if r == 0:
            for copy in edge_copies:
                copy.wait()
            last = (nx - 1) * ny
            low = spread_obs(edge[1].astype(BF16), edge_obs[0, rounds : rounds + 1], last, ny)
            high = spread_obs(edge[2].astype(BF16), edge_obs[1, rounds : rounds + 1], 0, ny)
            u = dot(weight[t], stacked(jnp.concatenate([low, high], axis=1)))
            field[:, 0:ny] += nu * u[:, 0:ny]
            field[:, last:] += nu * u[:, ny:]
        for copy in pending:
            copy.wait()
        acc = q_ref[r, 0]
        for j in range(1, members):
            acc = acc + q_ref[r, j]
        total[...] = acc
        smooth = stacked(smoothed(r))
        smooth = jnp.concatenate([smooth, jnp.zeros((pad, nx * ny), BF16)], axis=0)
        lifted = dot(lift_w[...], smooth)
        for x in range(nx):
            cols = slice(x * ny, (x + 1) * ny)
            field[:, cols] += anom32[pl.ds(x, state, stride=nx), :] * lifted[:, cols]
        if r > 0:
            for copy in halo:
                copy.wait()
            field[:, 0:ny] += nu * u_ref[r, 0]
            field[:, (nx - 1) * ny :] += nu * u_ref[r, nx + 1]
    for x in range(nx):
        out_ref[pl.ds(x, state, stride=nx), :] = field[:, x * ny : (x + 1) * ny]


def per_device(members, tiles, innovations, obs_column, physics, diffusion, anomalies, modes, bands):
    _, steps, state, obs = innovations.shape
    _, _, nx, ny = anomalies.shape
    count = modes.shape[1]
    rounds = steps - 1
    vmem = pl.BlockSpec(memory_space=pltpu.VMEM)
    hbm = pl.BlockSpec(memory_space=pl.ANY)
    out = pl.pallas_call(
        functools.partial(kernel, members, tiles),
        out_shape=jax.ShapeDtypeStruct((state * nx, ny), F32),
        in_specs=[pl.BlockSpec(memory_space=pltpu.SMEM), vmem, vmem, vmem, hbm, hbm, hbm],
        out_specs=vmem,
        scratch_shapes=[
            pltpu.VMEM((rounds, state, state), F32),
            pltpu.VMEM((steps, obs, state), BF16),
            pltpu.VMEM((state * nx, ny), BF16),
            pltpu.VMEM((state * nx, ny), F32),
            pltpu.VMEM((rounds, state, 3 * state), BF16),
            pltpu.VMEM((state, nx * ny), F32),
            pltpu.VMEM((state, ny), F32),
            pltpu.VMEM((state, ny), BF16),
            pltpu.VMEM((2 * count, state), BF16),
            pltpu.VMEM((2 * REACH + 1, count, ny), F32),
            pltpu.VMEM((3, obs, state), F32),
            pltpu.VMEM((2, steps, obs), jnp.int32),
            pltpu.VMEM((rounds, nx + 2, state, ny), F32),
            pltpu.VMEM((rounds, members, count, nx * ny), F32),
            pltpu.VMEM((count, nx * ny), F32),
            pltpu.SemaphoreType.DMA((3,)),
            pltpu.SemaphoreType.DMA((2,)),
            pltpu.SemaphoreType.DMA((2,)),
            pltpu.SemaphoreType.DMA((2,)),
            pltpu.SemaphoreType.DMA((2,)),
            pltpu.SemaphoreType.DMA((rounds, 2)),
            pltpu.SemaphoreType.DMA((rounds, 2)),
            pltpu.SemaphoreType.DMA((rounds, members)),
            pltpu.SemaphoreType.DMA((rounds, members)),
        ],
        compiler_params=pltpu.CompilerParams(
            collective_id=0, has_side_effects=True, vmem_limit_bytes=40 * 1024 * 1024
        ),
    )(
        bands, obs_column, diffusion.reshape(1, state), modes.T, physics,
        innovations.swapaxes(2, 3),
        anomalies.reshape(state * nx, ny),
    )
    return out.reshape(1, state, nx, ny)


def solution(mesh):
    in_specs = (
        P("member", None, None, "tile"),
        P(None, "tile"),
        P(),
        P(),
        P("member", None, "tile", None),
        P(),
        P(),
    )
    out_specs = P("member", None, "tile", None)
    return jax.shard_map(
        functools.partial(per_device, mesh.shape["member"], mesh.shape["tile"]),
        mesh=mesh, in_specs=in_specs, out_specs=out_specs, check_vma=False,
    )
```

time: 126 us -> 34.1 us (0.27)
  blocking collectives: 92.3 us -> 0 us
  Pallas kernels: 0 us -> 28.5 us
  starting transfers between devices: 15.3 us -> 0 us
  matrix products: 14 us -> 0 us
  local copies, waits for them, and re-layouts: 3.34 us -> 5.29 us
    psum x4 -> x0, blocking collectives: 92.3 us -> none  [per_device(): coeffs = lax.psum(local, 'member') / jnp.float32(members - 1)]
    pallas_call x0 -> x1, Pallas kernels: none -> 28.5 us  [per_device(): pl.pallas_call(functools.partial(kernel, members, tiles), out_shape=jax.S...]
    ppermute x8 -> x0, starting transfers between devices: 15.3 us -> none  [the longest x4 15.3 us: padded_2(): lax.ppermute(lax.slice_in_dim(block, 0, width, axis=dim), axis, backward)]
    dot_general x16 -> x0, matrix products: 14 us -> none  [the longest x4 7.03 us: per_device(): jnp.einsum('sk,kxy->sxy', modes, smooth, precision=lax.Precision.HIGHEST)]
    unnamed x19 -> x15, local copies, waits for them, and re-layouts: 1.55 us -> 5.29 us
  transfers between devices with their start and end apart: 8 -> 0, of which waited for: 0 -> 0; matrix products, arithmetic and copies ran while one was open for 2% -> 0% of each run, Pallas kernels for 0% -> 0%
where the time goes in v1:
time: 34.1 us; the launch traced here: 33.8 us
  Pallas kernels  28.5 us (84%)
  local copies, waits for them, and re-layouts  5.29 us (16%)
    pallas_call x1, Pallas kernels, per_device(): pl.pallas_call(functools.partial(kernel, members, tiles), out_shape=jax.S...  28.5 us
    unnamed x15, local copies, waits for them, and re-layouts  5.29 us

profile of v1, /device:TPU:0, one launch (start us, length us, event | category | flops | bytes accessed | tf_op | source)
XLA Modules:
  0.0 33.8 jit_solution(12898728294011409921)
XLA Ops:
  0.0 0.0 copy-start.4
  0.0 0.0 copy-start.5
  0.0 0.0 copy-start.6
  0.0 0.7 %copy-done.4 = s32[4,64]{1,0:T(4,128)S(1)} copy-done((s32[4,64]{1,0:T(4,128)S(1)}, s32[4,64]{1,0:T(4,128)}, u32[]{:S(2)}) %copy-start.4) | copy-done | bytes 1048
  0.7 0.0 copy-done.5
  0.7 0.0 copy-done.6
  0.7 0.0 copy-start
  0.7 1.2 %copy-done = f32[4,256,256]{2,1,0:T(8,128)S(1)} copy-done((f32[4,256,256]{2,1,0:T(8,128)S(1)}, f32[4,256,256]{2,1,0:T(8,128)}, u32[]{:S(2)}) %copy-start) | copy-done | bytes 1048600
  1.9 0.0 copy-start.1
  1.9 0.9 %copy-done.1 = bf16[1,256,4,128]{3,2,1,0:T(4,128)(2,1)S(1)} copy-done((bf16[1,256,4,128]{3,2,1,0:T(4,128)(2,1)S(1)}, bf16[1,256,4,128]{3,2,1,0:T(4,128)(2,1)}, u32[]{:S(2)}) %copy-start.1) | copy-done | bytes 262168
  2.9 0.0 copy-start.2
  2.9 0.9 %copy-done.2 = bf16[1,4,256,64]{2,3,1,0:T(8,128)(2,1)S(1)} copy-done((bf16[1,4,256,64]{2,3,1,0:T(8,128)(2,1)S(1)}, bf16[1,4,256,64]{2,3,1,0:T(8,128)(2,1)}, u32[]{:S(2)}) %copy-start.2) | copy-done | bytes 131096
  3.8 0.0 copy-start.3
  3.8 0.7 %copy-done.3 = f32[256,16]{0,1:T(8,128)S(1)} copy-done((f32[256,16]{0,1:T(8,128)S(1)}, f32[256,16]{0,1:T(8,128)}, u32[]{:S(2)}) %copy-start.3) | copy-done | bytes 16408
  4.5 28.5 %shard_map.73 = f32[1024,128]{1,0:T(8,128)S(1)} custom-call(s32[16]{0:T(128)S(1)} %copy-done.6, s32[4,64]{1,0:T(4,128)S(1)} %copy-done.4, f32[1,256]{1,0:T(1,128)S(1)} %bitcast.9, f32[16,256]{1,0:T(8,128)S(1)} %bitcast.8, f32[4,256,256]{2,1,0:T(8,128)S(1)} %copy-done, bf16[1,4,64,256]{3,2,1,0:T(8,128)(2,1)S(1)} %bitcast.7, bf16[1024,128]{1,0:T(8,128)(2,1)S(1)} %bitcast.6), custom_call_target="tpu_custom_call" | custom-call | tf_op jit(solution)/shard_map/pallas_call | solution.py:229
  33.0 0.8 %copy.9 = f32[1,256,4,128]{3,2,1,0:T(4,128)} copy(f32[1,256,4,128]{3,2,1,0:T(4,128)S(1)} %bitcast.5) | data formatting | bytes 1048576
Async XLA Ops:
  0.0 0.7 %copy-start.4 = (s32[4,64]{1,0:T(4,128)S(1)}, s32[4,64]{1,0:T(4,128)}, u32[]{:S(2)}) copy-start(s32[4,64]{1,0:T(4,128)} %obs_ref.1) | copy-start | bytes 3076
  0.0 0.7 %copy-start.5 = (f32[256]{0:T(256)S(1)}, f32[256]{0:T(256)}, u32[]{:S(2)}) copy-start(f32[256]{0:T(256)} %param.10) | copy-start | bytes 3076
  0.0 0.7 %copy-start.6 = (s32[16]{0:T(128)S(1)}, s32[16]{0:T(128)}, u32[]{:S(2)}) copy-start(s32[16]{0:T(128)} %bands_ref.1) | copy-start | bytes 196
  0.7 1.2 %copy-start = (f32[4,256,256]{2,1,0:T(8,128)S(1)}, f32[4,256,256]{2,1,0:T(8,128)}, u32[]{:S(2)}) copy-start(f32[4,256,256]{2,1,0:T(8,128)} %phys_ref.1) | copy-start | bytes 3145732
  1.9 0.9 %copy-start.1 = (bf16[1,256,4,128]{3,2,1,0:T(4,128)(2,1)S(1)}, bf16[1,256,4,128]{3,2,1,0:T(4,128)(2,1)}, u32[]{:S(2)}) copy-start(bf16[1,256,4,128]{3,2,1,0:T(4,128)(2,1)} %param.11) | copy-start | bytes 786436
  2.9 0.9 %copy-start.2 = (bf16[1,4,256,64]{2,3,1,0:T(8,128)(2,1)S(1)}, bf16[1,4,256,64]{2,3,1,0:T(8,128)(2,1)}, u32[]{:S(2)}) copy-start(bf16[1,4,256,64]{2,3,1,0:T(8,128)(2,1)} %param.7) | copy-start | bytes 393220
  3.8 0.7 %copy-start.3 = (f32[256,16]{0,1:T(8,128)S(1)}, f32[256,16]{0,1:T(8,128)}, u32[]{:S(2)}) copy-start(f32[256,16]{0,1:T(8,128)} %param.12) | copy-start | bytes 49156

commit v2 on v1

--- a/solution.py
+++ b/solution.py
@@ -37,9 +37,9 @@
 
 
 def kernel(
-    members, tiles, bands_ref, obs_ref, diff_ref, modes_ref, phys_ref, innov_ref, anom_ref,
+    members, tiles, bands_hbm, obs_hbm, diff_hbm, modes_hbm, phys_ref, innov_ref, anom_ref,
     out_ref,
-    phys, innov, anom, anom32, weight, field, nu_ref, lift_w, proj_w, smooth_w,
+    bands_ref, obs_ref, diff_ref, modes_ref, phys, innov, anom, anom32, weight, field, nu_ref, lift_w, proj_w, smooth_w,
     edge, edge_obs, u_ref, q_ref, total,
     local_sem, edge_send, edge_recv, obs_send, obs_recv, u_send, u_recv, q_send, q_recv,
 ):
@@ -56,9 +56,12 @@
     get_innov = pltpu.make_async_copy(innov_ref.at[0], innov, local_sem.at[0])
     get_phys = pltpu.make_async_copy(phys_ref.at[pl.ds(0, rounds)], phys, local_sem.at[1])
     get_anom = pltpu.make_async_copy(anom_ref, anom, local_sem.at[2])
-    get_innov.start()
-    get_anom.start()
-    get_phys.start()
+    get_obs = pltpu.make_async_copy(obs_hbm, obs_ref, local_sem.at[3])
+    get_modes = pltpu.make_async_copy(modes_hbm, modes_ref, local_sem.at[4])
+    get_bands = pltpu.make_async_copy(bands_hbm, bands_ref, local_sem.at[5])
+    get_diff = pltpu.make_async_copy(diff_hbm, diff_ref, local_sem.at[6])
+    for get in (get_innov, get_obs, get_modes, get_anom, get_phys, get_bands, get_diff):
+        get.start()
 
     barrier = pltpu.get_barrier_semaphore()
     for near in (before, after):
@@ -69,6 +72,7 @@
 
     get_innov.wait()
     edge[0] = innov[rounds].astype(F32)
+    get_obs.wait()
     pl.semaphore_wait(barrier, members + 1)
 
     edge_copies = []
@@ -85,6 +89,7 @@
     obs_all = obs_ref[...]
     field[...] = spread_obs(innov[rounds], obs_all[rounds : rounds + 1], 0, nx * ny)
 
+    get_modes.wait()
     hi, lo = split(modes_ref[...])
     proj_w[...] = jnp.concatenate([hi, lo], axis=0)
     parts = jnp.concatenate([hi, hi, lo], axis=0).astype(F32)
@@ -118,6 +123,7 @@
     row = lax.broadcasted_iota(jnp.int32, (modes, ny), 0)
     lane = lax.broadcasted_iota(jnp.int32, (modes, ny), 1)
     bands = jnp.zeros((modes, ny), jnp.int32)
+    get_bands.wait()
     for k in range(modes):
         bands = jnp.where(row == k, bands_ref[k], bands)
     scale = 1.0 / ((2 * bands + 1).astype(F32) * F32(members - 1))
@@ -125,6 +131,7 @@
         ok = (abs(d) <= bands) & (lane + d >= 0) & (lane + d < ny)
         smooth_w[i] = jnp.where(ok, scale, 0.0)
 
+    get_diff.wait()
     nu_ref[...] = jnp.broadcast_to(diff_ref[...], (ny, state)).T
 
     get_phys.wait()
@@ -229,9 +236,13 @@
     out = pl.pallas_call(
         functools.partial(kernel, members, tiles),
         out_shape=jax.ShapeDtypeStruct((state * nx, ny), F32),
-        in_specs=[pl.BlockSpec(memory_space=pltpu.SMEM), vmem, vmem, vmem, hbm, hbm, hbm],
+        in_specs=[hbm] * 7,
         out_specs=vmem,
         scratch_shapes=[
+            pltpu.SMEM((count,), jnp.int32),
+            pltpu.VMEM((steps, obs), jnp.int32),
+            pltpu.VMEM((1, state), F32),
+            pltpu.VMEM((count, state), F32),
             pltpu.VMEM((rounds, state, state), F32),
             pltpu.VMEM((steps, obs, state), BF16),
             pltpu.VMEM((state * nx, ny), BF16),
@@ -247,7 +258,7 @@
             pltpu.VMEM((rounds, nx + 2, state, ny), F32),
             pltpu.VMEM((rounds, members, count, nx * ny), F32),
             pltpu.VMEM((count, nx * ny), F32),
-            pltpu.SemaphoreType.DMA((3,)),
+            pltpu.SemaphoreType.DMA((7,)),
             pltpu.SemaphoreType.DMA((2,)),
             pltpu.SemaphoreType.DMA((2,)),
             pltpu.SemaphoreType.DMA((2,)),
@@ -258,7 +269,7 @@
             pltpu.SemaphoreType.DMA((rounds, members)),
         ],
         compiler_params=pltpu.CompilerParams(
-            collective_id=0, has_side_effects=True, vmem_limit_bytes=40 * 1024 * 1024
+            collective_id=0, has_side_effects=True, vmem_limit_bytes=60 * 1024 * 1024
         ),
     )(
         bands, obs_column, diffusion.reshape(1, state), modes.T, physics,

time: 34.1 us -> 30.6 us (0.90)
  local copies, waits for them, and re-layouts: 5.29 us -> 1.87 us
    unnamed x15 -> x1, local copies, waits for them, and re-layouts: 5.29 us -> 1.87 us
where the time goes in v2:
time: 30.6 us; the launch traced here: 30.4 us
  Pallas kernels  28.5 us (93%)
  local copies, waits for them, and re-layouts  1.87 us (6%)
    pallas_call x1, Pallas kernels, per_device(): pl.pallas_call(functools.partial(kernel, members, tiles), out_shape=jax.S...  28.5 us
    unnamed x1, local copies, waits for them, and re-layouts  1.87 us

profile of v2, /device:TPU:0, one launch (start us, length us, event | category | flops | bytes accessed | tf_op | source)
XLA Modules:
  0.0 30.4 jit_solution(14922648529138550157)
XLA Ops:
  0.0 28.5 %shard_map.73 = f32[1024,128]{1,0:T(8,128)} custom-call(s32[16]{0:T(128)} %bands_hbm.1, s32[4,64]{1,0:T(4,128)} %obs_hbm.1, f32[1,256]{1,0:T(1,128)} %bitcast.9, f32[16,256]{1,0:T(8,128)} %bitcast.8, f32[4,256,256]{2,1,0:T(8,128)} %phys_ref.1, bf16[1,4,64,256]{3,2,1,0:T(8,128)(2,1)} %bitcast.7, bf16[1024,128]{1,0:T(8,128)(2,1)} %bitcast.6), custom_call_target="tpu_custom_call" | custom-call | tf_op jit(solution)/shard_map/pallas_call | solution.py:236
  28.5 1.9 %copy.9 = f32[1,256,4,128]{3,2,1,0:T(4,128)} copy(f32[1,256,4,128]{3,2,1,0:T(4,128)} %bitcast.5) | data formatting | bytes 1048576

commit v3 on v2

--- a/solution.py
+++ b/solution.py
@@ -40,7 +40,7 @@
     members, tiles, bands_hbm, obs_hbm, diff_hbm, modes_hbm, phys_ref, innov_ref, anom_ref,
     out_ref,
     bands_ref, obs_ref, diff_ref, modes_ref, phys, innov, anom, anom32, weight, field, nu_ref, lift_w, proj_w, smooth_w,
-    edge, edge_obs, u_ref, q_ref, total,
+    edge, edge_obs, u_ref, halo_out, halo_in, q_ref, total,
     local_sem, edge_send, edge_recv, obs_send, obs_recv, u_send, u_recv, q_send, q_recv,
 ):
     steps, obs, state = innov.shape
@@ -156,26 +156,40 @@
 
     lane_y = lax.broadcasted_iota(jnp.int32, (state, ny), 1)
 
+    half = ny // 2
+    lower = lax.broadcasted_iota(jnp.int32, (state, ny), 1) < half
+    last = (nx - 1) * ny
+    unsent = []
+
+    def trade(a, b):
+        keep = lower[0 : a.shape[0]]
+        first = jnp.where(keep, a, pltpu.roll(b, half, 1))
+        return first, jnp.where(keep, pltpu.roll(a, half, 1), b)
+
+    def send_part(r, part, layers):
+        u = dot(weight[rounds - 1 - r], stacked(layers))
+        left, right = trade(u[0 : state // 2], u[state // 2 :])
+        halo_out[r, part, 0] = left
+        halo_out[r, part, 1] = right
+        copies = [
+            pltpu.make_async_remote_copy(
+                halo_out.at[r, part, side], halo_in.at[r, part, 1 - side],
+                u_send.at[r, part, side], u_recv.at[r, part, 1 - side],
+                device_id={"tile": near}, device_id_type=MESH)
+            for side, near in ((0, before), (1, after))
+        ]
+        for copy in copies:
+            copy.start()
+        unsent.extend(copies)
+        return u, copies
+
+    sent = []
     for r in range(rounds):
         t = rounds - 1 - r
-        halo = []
         if r > 0:
-            outer = jnp.concatenate([field[:, 0:ny], field[:, (nx - 1) * ny :]], axis=1)
-            u = dot(weight[t], stacked(outer))
-            u_ref[r, 1] = u[:, 0:ny]
-            u_ref[r, nx] = u[:, ny:]
-            halo = [
-                pltpu.make_async_remote_copy(
-                    u_ref.at[r, 1], u_ref.at[r, nx + 1], u_send.at[r, 0], u_recv.at[r, 0],
-                    device_id={"tile": before}, device_id_type=MESH),
-                pltpu.make_async_remote_copy(
-                    u_ref.at[r, nx], u_ref.at[r, 0], u_send.at[r, 1], u_recv.at[r, 1],
-                    device_id={"tile": after}, device_id_type=MESH),
-            ]
-            for copy in halo:
-                copy.start()
             pending = project_and_send(r)
-            u = dot(weight[t], stacked(field[:, ny : (nx - 1) * ny]))
+            u_ref[r, 1], u_ref[r, nx] = trade(sent[0][0], sent[1][0])
+            u = dot(weight[t], stacked(field[:, ny:last]))
             for x in range(1, nx - 1):
                 u_ref[r, 1 + x] = u[:, (x - 1) * ny : x * ny]
         else:
@@ -199,7 +213,6 @@
         if r == 0:
             for copy in edge_copies:
                 copy.wait()
-            last = (nx - 1) * ny
             low = spread_obs(edge[1].astype(BF16), edge_obs[0, rounds : rounds + 1], last, ny)
             high = spread_obs(edge[2].astype(BF16), edge_obs[1, rounds : rounds + 1], 0, ny)
             u = dot(weight[t], stacked(jnp.concatenate([low, high], axis=1)))
@@ -217,11 +230,20 @@
         for x in range(nx):
             cols = slice(x * ny, (x + 1) * ny)
             field[:, cols] += anom32[pl.ds(x, state, stride=nx), :] * lifted[:, cols]
+        layers = list(trade(field[:, 0:ny], field[:, last:]))
+        arriving, sent = sent, []
+        for part in range(2):
+            if r > 0:
+                for copy in arriving[part][1]:
+                    copy.wait_recv()
+                outside = trade(halo_in[r, part, 0], halo_in[r, part, 1])
+                layers[part] = layers[part] + nu * jnp.concatenate(outside, axis=0)
+            if r < rounds - 1:
+                sent.append(send_part(r + 1, part, layers[part]))
         if r > 0:
-            for copy in halo:
-                copy.wait()
-            field[:, 0:ny] += nu * u_ref[r, 0]
-            field[:, (nx - 1) * ny :] += nu * u_ref[r, nx + 1]
+            field[:, 0:ny], field[:, last:] = trade(*layers)
+    for copy in unsent:
+        copy.wait_send()
     for x in range(nx):
         out_ref[pl.ds(x, state, stride=nx), :] = field[:, x * ny : (x + 1) * ny]
 
@@ -256,6 +278,8 @@
             pltpu.VMEM((3, obs, state), F32),
             pltpu.VMEM((2, steps, obs), jnp.int32),
             pltpu.VMEM((rounds, nx + 2, state, ny), F32),
+            pltpu.VMEM((rounds, 2, 2, state // 2, ny), F32),
+            pltpu.VMEM((rounds, 2, 2, state // 2, ny), F32),
             pltpu.VMEM((rounds, members, count, nx * ny), F32),
             pltpu.VMEM((count, nx * ny), F32),
             pltpu.SemaphoreType.DMA((7,)),
@@ -263,8 +287,8 @@
             pltpu.SemaphoreType.DMA((2,)),
             pltpu.SemaphoreType.DMA((2,)),
             pltpu.SemaphoreType.DMA((2,)),
-            pltpu.SemaphoreType.DMA((rounds, 2)),
-            pltpu.SemaphoreType.DMA((rounds, 2)),
+            pltpu.SemaphoreType.DMA((rounds, 2, 2)),
+            pltpu.SemaphoreType.DMA((rounds, 2, 2)),
             pltpu.SemaphoreType.DMA((rounds, members)),
             pltpu.SemaphoreType.DMA((rounds, members)),
         ],

time: 30.6 us -> 30.1 us (0.984)
  Pallas kernels: 28.5 us -> 28 us
    pallas_call x1, Pallas kernels: 28.5 us -> 28 us  [per_device(): pl.pallas_call(functools.partial(kernel, members, tiles), out_shape=jax.S...]
where the time goes in v3:
time: 30.1 us; the launch traced here: 29.9 us
  Pallas kernels  28 us (93%)
  local copies, waits for them, and re-layouts  1.87 us (6%)
    pallas_call x1, Pallas kernels, per_device(): pl.pallas_call(functools.partial(kernel, members, tiles), out_shape=jax.S...  28 us
    unnamed x1, local copies, waits for them, and re-layouts  1.87 us

profile of v3, /device:TPU:0, one launch (start us, length us, event | category | flops | bytes accessed | tf_op | source)
XLA Modules:
  0.0 29.9 jit_solution(8675253464665962010)
XLA Ops:
  0.0 28.0 %shard_map.73 = f32[1024,128]{1,0:T(8,128)} custom-call(s32[16]{0:T(128)} %bands_hbm.1, s32[4,64]{1,0:T(4,128)} %obs_hbm.1, f32[1,256]{1,0:T(1,128)} %bitcast.9, f32[16,256]{1,0:T(8,128)} %bitcast.8, f32[4,256,256]{2,1,0:T(8,128)} %phys_ref.1, bf16[1,4,64,256]{3,2,1,0:T(8,128)(2,1)} %bitcast.7, bf16[1024,128]{1,0:T(8,128)(2,1)} %bitcast.6), custom_call_target="tpu_custom_call" | custom-call | tf_op jit(solution)/shard_map/pallas_call | solution.py:258
  28.1 1.9 %copy.9 = f32[1,256,4,128]{3,2,1,0:T(4,128)} copy(f32[1,256,4,128]{3,2,1,0:T(4,128)} %bitcast.5) | data formatting | bytes 1048576

commit v4 on v3

--- a/solution.py
+++ b/solution.py
@@ -40,14 +40,15 @@
     members, tiles, bands_hbm, obs_hbm, diff_hbm, modes_hbm, phys_ref, innov_ref, anom_ref,
     out_ref,
     bands_ref, obs_ref, diff_ref, modes_ref, phys, innov, anom, anom32, weight, field, nu_ref, lift_w, proj_w, smooth_w,
-    edge, edge_obs, u_ref, halo_out, halo_in, q_ref, total,
-    local_sem, edge_send, edge_recv, obs_send, obs_recv, u_send, u_recv, q_send, q_recv,
+    edge, edge_obs, u_ref, halo_out, halo_in, own, q_ref, total,
+    local_sem, edge_send, edge_recv, obs_send, obs_recv, u_send, u_recv, q_send, q_recv, t_send, t_recv,
 ):
     steps, obs, state = innov.shape
     ny = anom.shape[1]
     nx = anom.shape[0] // state
     modes = modes_ref.shape[0]
     rounds = steps - 1
+    share = modes * nx // members
     me = lax.axis_index("member")
     tile = lax.axis_index("tile")
     after = lax.rem(tile + 1, tiles)
@@ -108,15 +109,32 @@
             lo_cols.append(b)
         both = dot(proj_w[...], jnp.concatenate(hi_cols, axis=1))
         low = dot(proj_w[0:modes], jnp.concatenate(lo_cols, axis=1))
-        q_ref[r, 0] = both[0:modes] + both[modes:] + low
+        q = both[0:modes] + both[modes:] + low
+        q = jnp.concatenate([q[:, x * ny : (x + 1) * ny] for x in range(nx)], axis=0)
+        for m in range(members):
+            own[r, m] = q[m * share : (m + 1) * share]
+        return to_peers(lambda peer, j: (own.at[r, peer], q_ref.at[r, j]), q_send.at[r], q_recv.at[r])
+
+    def to_peers(refs, send, recv):
         copies = []
         for j in range(1, members):
+            peer = lax.rem(me + j, members)
+            src, dst = refs(peer, j)
             copies.append(pltpu.make_async_remote_copy(
-                q_ref.at[r, 0], q_ref.at[r, j], q_send.at[r, j], q_recv.at[r, j],
-                device_id={"member": lax.rem(me + j, members)}, device_id_type=MESH))
+                src, dst, send.at[j], recv.at[j],
+                device_id={"member": peer}, device_id_type=MESH))
         for copy in copies:
             copy.start()
         return copies
+
+    def add_and_return(r, copies):
+        for copy in copies:
+            copy.wait()
+        acc = own[r, me]
+        for j in range(1, members):
+            acc = acc + q_ref[r, j]
+        total[r, me] = acc
+        return to_peers(lambda peer, j: (total.at[r, me], total.at[r, me]), t_send.at[r], t_recv.at[r])
 
     pending = project_and_send(0)
 
@@ -144,9 +162,9 @@
 
     def smoothed(r):
         rows = []
+        sums = jnp.concatenate([total[r, m] for m in range(members)], axis=0)
         for x in range(nx):
-            cols = slice(x * ny, (x + 1) * ny)
-            q = total[:, cols]
+            q = sums[x * modes : (x + 1) * modes]
             acc = smooth_w[REACH] * q
             for i, d in enumerate(range(-REACH, REACH + 1)):
                 if d != 0:
@@ -196,6 +214,7 @@
             u = dot(weight[t], stacked(field[...]))
             for x in range(nx):
                 u_ref[r, 1 + x] = u[:, x * ny : (x + 1) * ny]
+        pending = add_and_return(r, pending)
         if t > 0:
             physics_weights(t - 1)
         nu = nu_ref[...]
@@ -220,10 +239,6 @@
             field[:, last:] += nu * u[:, ny:]
         for copy in pending:
             copy.wait()
-        acc = q_ref[r, 0]
-        for j in range(1, members):
-            acc = acc + q_ref[r, j]
-        total[...] = acc
         smooth = stacked(smoothed(r))
         smooth = jnp.concatenate([smooth, jnp.zeros((pad, nx * ny), BF16)], axis=0)
         lifted = dot(lift_w[...], smooth)
@@ -280,8 +295,9 @@
             pltpu.VMEM((rounds, nx + 2, state, ny), F32),
             pltpu.VMEM((rounds, 2, 2, state // 2, ny), F32),
             pltpu.VMEM((rounds, 2, 2, state // 2, ny), F32),
-            pltpu.VMEM((rounds, members, count, nx * ny), F32),
-            pltpu.VMEM((count, nx * ny), F32),
+            pltpu.VMEM((rounds, members, count * nx // members, ny), F32),
+            pltpu.VMEM((rounds, members, count * nx // members, ny), F32),
+            pltpu.VMEM((rounds, members, count * nx // members, ny), F32),
             pltpu.SemaphoreType.DMA((7,)),
             pltpu.SemaphoreType.DMA((2,)),
             pltpu.SemaphoreType.DMA((2,)),
@@ -289,6 +305,8 @@
             pltpu.SemaphoreType.DMA((2,)),
             pltpu.SemaphoreType.DMA((rounds, 2, 2)),
             pltpu.SemaphoreType.DMA((rounds, 2, 2)),
+            pltpu.SemaphoreType.DMA((rounds, members)),
+            pltpu.SemaphoreType.DMA((rounds, members)),
             pltpu.SemaphoreType.DMA((rounds, members)),
             pltpu.SemaphoreType.DMA((rounds, members)),
         ],

time: 30.1 us -> 33.7 us (1.12)
  Pallas kernels: 28 us -> 31.6 us
    pallas_call x1, Pallas kernels: 28 us -> 31.6 us  [per_device(): pl.pallas_call(functools.partial(kernel, members, tiles), out_shape=jax.S...]
where the time goes in v4:
time: 33.7 us; the launch traced here: 33.5 us
  Pallas kernels  31.6 us (94%)
  local copies, waits for them, and re-layouts  1.87 us (6%)
    pallas_call x1, Pallas kernels, per_device(): pl.pallas_call(functools.partial(kernel, members, tiles), out_shape=jax.S...  31.6 us
    unnamed x1, local copies, waits for them, and re-layouts  1.87 us

profile of v4, /device:TPU:0, one launch (start us, length us, event | category | flops | bytes accessed | tf_op | source)
XLA Modules:
  0.0 33.5 jit_solution(1551076145621863525)
XLA Ops:
  0.0 31.6 %shard_map.73 = f32[1024,128]{1,0:T(8,128)} custom-call(s32[16]{0:T(128)} %bands_hbm.1, s32[4,64]{1,0:T(4,128)} %obs_hbm.1, f32[1,256]{1,0:T(1,128)} %bitcast.9, f32[16,256]{1,0:T(8,128)} %bitcast.8, f32[4,256,256]{2,1,0:T(8,128)} %phys_ref.1, bf16[1,4,64,256]{3,2,1,0:T(8,128)(2,1)} %bitcast.7, bf16[1024,128]{1,0:T(8,128)(2,1)} %bitcast.6), custom_call_target="tpu_custom_call" | custom-call | tf_op jit(solution)/shard_map/pallas_call | solution.py:273
  31.6 1.9 %copy.9 = f32[1,256,4,128]{3,2,1,0:T(4,128)} copy(f32[1,256,4,128]{3,2,1,0:T(4,128)} %bitcast.5) | data formatting | bytes 1048576
